TPU v7x, 256 devices: a whole 4x4x8 slice. The times are simulated.
256 devices in a mesh: fsdp: 16 (over x, y), tp: 16 (over z, core).
Axes of the slice: x: 4, y: 4, z: 8, core: 2. Of those that a mesh axis runs over, the one named last changes fastest.
Arguments:
- momentum: bfloat16 [8192, 26624], P('fsdp', 'tp'), may hold values from -6 to 6
- gradient: bfloat16 [8192, 26624], P('fsdp', 'tp'), may hold values from -3 to 3
- basis: bfloat16 [26624, 256], P('tp'), may hold values from -0.010663815 to 0.010663815
Outputs:
- momentum_next: bfloat16 [8192, 26624], P('fsdp', 'tp')
- basis_next: bfloat16 [26624, 256], P('tp')
- update: bfloat16 [8192, 26624], P('fsdp', 'tp')
All inputs are finite; a program needn't handle non-finite values.
Results may differ from a plain program's by a relative error of at most 0.009.
Values may be sent and summed in bfloat16 or wider, within the bound.
No kernel may reach another device: no remote copies, remote signals or barrier semaphores. Data moves between devices by JAX's collectives and lax.ppermute only.
A program may use at most 64 MiB of HBM per device.

v0:
```python
import jax
import jax.numpy as jnp
from jax import lax
from jax.sharding import PartitionSpec as P

M_ROWS = 8192
N_COLS = 26624
RANK = 256


def orthonormal(left_rows, gram):
    gram = gram + 0.001 * jnp.eye(gram.shape[0], dtype=jnp.float32)
    factor = jnp.linalg.cholesky(gram)
    return lax.linalg.triangular_solve(
        factor, left_rows, left_side=False, lower=True, transpose_a=True
    ).astype(jnp.bfloat16)


def on_device(momentum, gradient, basis):
    blended = (momentum.astype(jnp.float32) + gradient.astype(jnp.float32)).astype(jnp.bfloat16)
    left = lax.psum(jnp.dot(blended, basis, preferred_element_type=jnp.float32), "tp")
    gram = lax.psum(
        jnp.dot(left.T, left, precision=lax.Precision.HIGHEST, preferred_element_type=jnp.float32),
        "fsdp",
    )
    ortho = orthonormal(left, gram)
    right = lax.psum(
        lax.dot_general(
            blended, ortho, (((0,), (0,)), ((), ())), preferred_element_type=jnp.float32
        ),
        "fsdp",
    )
    colsq = lax.psum(jnp.sum(right * right, axis=0), "tp")
    basis_next = (right * lax.rsqrt(colsq + 1e-06)).astype(jnp.bfloat16)
    right_low = right.astype(jnp.bfloat16)
    feedback = lax.dot_general(
        ortho, right_low, (((1,), (1,)), ((), ())), preferred_element_type=jnp.float32
    )
    momentum_next = (blended.astype(jnp.float32) - 0.1 * feedback).astype(jnp.bfloat16)
    scale = (M_ROWS * N_COLS / RANK) ** 0.5
    product = lax.dot_general(
        ortho, basis_next, (((1,), (1,)), ((), ())), preferred_element_type=jnp.float32
    )
    update = (scale * product).astype(jnp.bfloat16)
    return (momentum_next, basis_next, update)


def solution(mesh):
    return jax.shard_map(
        on_device,
        mesh=mesh,
        in_specs=(P("fsdp", "tp"), P("fsdp", "tp"), P("tp", None)),
        out_specs=(P("fsdp", "tp"), P("tp", None), P("fsdp", "tp")),
        check_vma=False,
    )
```

profile of v0, /device:TPU:1, one launch (start us, length us, event | category | flops | bytes accessed | tf_op | source)
XLA Modules:
  0.0 429.5 jit_solution(15863793264973028504)
XLA Ops:
  7.2 0.0 copy-start
  7.2 0.0 all-reduce.5.cloned.1.call-start
  7.2 1.1 copy-done
  8.3 3.4 fusion.12
  11.7 0.0 all-reduce.5.cloned.1.call-update
  11.8 0.0 all-reduce.7.cloned.1.call-start
  11.8 113.5 %all-reduce.5.cloned.1.call-done = f32[512,256]{1,0:T(8,128)} async-done(((f32[512,256]{1,0:T(8,128)}), f32[512,256]{1,0:T(8,128)}) %all-reduce.5.cloned.1.call-update) | async-done | bytes 524304 | tf_op jit(solution)/shard_map/psum | solution.py:21
  125.3 2.9 fusion.15
  128.2 0.0 all-reduce.7.cloned.1.call-update
  128.2 0.0 all-reduce.9.cloned.1.call-start
  128.3 94.5 %all-reduce.7.cloned.1.call-done = f32[256,256]{0,1:T(8,128)} async-done(((f32[256,256]{0,1:T(8,128)}), f32[256,256]{0,1:T(8,128)}) %all-reduce.7.cloned.1.call-update) | async-done | bytes 262160 | tf_op jit(solution)/shard_map/psum | solution.py:22
  222.8 1.0 select_add_fusion
  223.8 0.1 copy.7
  224.0 1.0 fusion.3
  225.0 11.7 %cholesky.49 = f32[128,128]{1,0:T(8,128)S(1)} custom-call(f32[128,128]{1,0:T(8,128)S(1)} %cholesky.115), custom_call_target="Cholesky" | custom-call | tf_op jit(solution)/shard_map/jit(cholesky)/cholesky | solution.py:13
  236.7 0.1 copy.8
  236.8 9.8 %custom-call.14 = f32[1,128,128]{1,2,0:T(8,128)S(1)} custom-call(f32[1,128,128]{2,1,0:T(8,128)S(1)} %get-tuple-element.26), custom_call_target="InvertDiagBlocksLowerTriangular" | custom-call | tf_op jit(solution)/shard_map/jit(cholesky)/cholesky | solution.py:13
  246.6 0.2 fusion.6
  246.9 0.3 convolution_subtract_fusion.1
  247.1 0.1 copy.9
  247.2 11.7 %cholesky.103 = f32[128,128]{1,0:T(8,128)S(1)} custom-call(f32[128,128]{1,0:T(8,128)S(1)} %convolution_subtract_fusion.1), custom_call_target="Cholesky" | custom-call | tf_op jit(solution)/shard_map/jit(cholesky)/cholesky | solution.py:13
  259.0 0.0 copy-start.5
  259.0 0.1 copy.10
  259.1 0.7 compare_reduce_fusion
  261.2 0.1 triangular_solve.61
  261.3 0.0 copy-start.2
  261.3 5.7 %while.1 = (s32[]{:T(128)}, f32[256,256]{0,1:T(8,128)S(1)}, s32[2,2]{1,0:T(2,128)S(1)}, f32[2,128,128]{2,1,0:T(8,128)}, s32[]{:T(128)}) while((s32[]{:T(128)}, f32[256,256]{0,1:T(8,128)S(1)}, s32[2,2]{1,0:T(2,128)S(1)}, f32[2,128,128]{2,1,0:T(8,128)}, s32[]{:T(128)}) %tuple.27), condition=%wide.while_cond, body=%wide.while_body.sunk | while | flops 2 | bytes 393329 | solution.py:14
  261.5 0.6 fusion.25
  262.1 1.4 dynamic-slice.7
  263.5 0.1 copy.15
  263.6 0.6 bitcast_dynamic-update-slice_fusion.2
  264.2 0.6 fusion.25
  264.8 1.4 dynamic-slice.7
  266.3 0.1 copy.15
  266.4 0.6 bitcast_dynamic-update-slice_fusion.2
  267.0 20.5 %custom-call.15 = f32[2,128,128]{1,2,0:T(8,128)S(1)} custom-call(f32[2,128,128]{2,1,0:T(8,128)} %get-tuple-element.10), custom_call_target="InvertDiagBlocksLowerTriangular" | custom-call | tf_op jit(solution)/shard_map/triangular_solve | solution.py:14
  287.5 0.0 copy-done.5
  287.5 0.4 fusion.14
  287.9 0.0 copy-start.6
  288.0 0.6 convolution_subtract_fusion
  288.6 0.4 convolution_convert_fusion
  289.0 0.0 copy-done.6
  289.0 0.0 copy-done.2
  289.0 3.3 fusion.4
  292.3 0.0 all-reduce.9.cloned.1.call-update
  292.3 98.1 %all-reduce.9.cloned.1.call-done = f32[1664,256]{1,0:T(8,128)} async-done(((f32[1664,256]{1,0:T(8,128)}), f32[1664,256]{1,0:T(8,128)}) %all-reduce.9.cloned.1.call-update) | async-done | bytes 1703952 | tf_op jit(solution)/shard_map/psum | solution.py:27
  390.4 0.0 copy-start.1
  390.4 1.8 multiply_reduce_fusion
  392.3 0.0 copy-start.7
  392.3 25.7 %psum.31 = f32[256]{0:T(256)S(1)} all-reduce(f32[256]{0:T(256)S(1)} %multiply_reduce_fusion), channel_id=1, replica_groups=mesh['fsdp'=16,'tp'=16] {'tp'}, use_global_device_ids=true, to_apply=%region_8.9 | all-reduce | flops 256 | bytes 2048 | tf_op jit(solution)/shard_map/psum | solution.py:33
  417.9 0.0 copy-done.1
  417.9 0.0 copy-start.4
  417.9 0.1 multiply_convert_fusion.1
  418.1 0.0 copy-done.7
  418.1 0.0 copy-start.8
  418.1 0.0 copy-start.3
  418.1 1.9 multiply_convert_fusion
  420.0 0.0 copy-done.4
  420.0 0.8 copy-done.3
  420.8 2.1 subtract_convert_fusion
  422.9 0.0 copy-done.8
  (12 shorter events, 0.2 us)
Async XLA Ops:
  7.2 1.2 copy-start
  7.2 118.1 %all-reduce.5.cloned.1.call-start = ((), (), s32[]{:S(2)}) async-start(), calls=%async_computation | async-start | bytes 1048576 | tf_op jit(solution)/shard_map/psum | solution.py:21
  11.8 211.1 %all-reduce.7.cloned.1.call-start = ((), (), s32[]{:S(2)}) async-start(), calls=%async_computation.1 | async-start | bytes 524288 | tf_op jit(solution)/shard_map/psum | solution.py:22
  128.2 262.2 %all-reduce.9.cloned.1.call-start = ((), (), s32[]{:S(2)}) async-start(), calls=%async_computation.2 | async-start | bytes 3407872 | tf_op jit(solution)/shard_map/psum | solution.py:27
  259.0 28.5 %copy-start.5 = (f32[512,256]{1,0:T(8,128)S(1)}, f32[512,256]{1,0:T(8,128)}, u32[]{:S(2)}) copy-start(f32[512,256]{1,0:T(8,128)} %all-reduce.5.cloned.1.call-done) | copy-start | bytes 1572868
  261.3 27.7 %copy-start.2 = (bf16[512,1664]{1,0:T(8,128)(2,1)S(1)}, bf16[512,1664]{1,0:T(8,128)(2,1)}, u32[]{:S(2)}) copy-start(bf16[512,1664]{1,0:T(8,128)(2,1)} %param.4) | copy-start | bytes 5111812
  287.9 1.0 copy-start.6
  390.4 27.5 %copy-start.1 = (f32[1664,256]{1,0:T(8,128)S(1)}, f32[1664,256]{1,0:T(8,128)}, u32[]{:S(2)}) copy-start(f32[1664,256]{1,0:T(8,128)} %all-reduce.9.cloned.1.call-done) | copy-start | bytes 5111812
  392.3 25.8 %copy-start.7 = (bf16[512,128]{0,1:T(8,128)(2,1)S(1)}, bf16[512,128]{0,1:T(8,128)(2,1)}, u32[]{:S(2)}) copy-start(bf16[512,128]{0,1:T(8,128)(2,1)} %copy-done.6) | copy-start | bytes 393220
  417.9 2.1 copy-start.4
  418.1 4.8 %copy-start.8 = (bf16[1664,256]{1,0:T(8,128)(2,1)}, bf16[1664,256]{1,0:T(8,128)(2,1)S(1)}, u32[]{:S(2)}) copy-start(bf16[1664,256]{1,0:T(8,128)(2,1)S(1)} %multiply_convert_fusion.1) | copy-start | bytes 2555908
  418.1 2.7 copy-start.3
Sparse Core Ops, SparseCore 0:
  11.9 113.3 all-reduce.4
  129.4 93.4 all-reduce.6
  292.5 97.9 all-reduce.8
where the time goes:
time: 430 us; the launch traced here: 429 us
  waiting for transfers between devices  306 us (71%)
  other arithmetic  58.5 us (14%)
  blocking collectives  25.7 us (6%)
  matrix products  15.5 us (4%)
  between operations  15.3 us (4%)
  local copies, waits for them, and re-layouts  8.01 us (2%)
    psum x1, waiting for transfers between devices, on_device(): lax.psum(jnp.dot(blended, basis, preferred_element_type=jnp.float32), 'tp')  113 us
    psum x1, waiting for transfers between devices, on_device(): lax.psum(lax.dot_general(blended, ortho, (((0,), (0,)), ((), ())), prefer...  98.1 us
    psum x1, waiting for transfers between devices, on_device(): lax.psum(jnp.dot(left.T, left, precision=lax.Precision.HIGHEST, preferred...  94.5 us
    another operation x6, other arithmetic, orthonormal(): factor = jnp.linalg.cholesky(gram)  34 us
    psum x1, blocking collectives, on_device(): colsq = lax.psum(jnp.sum(right * right, axis=0), 'tp')  25.7 us
    another operation x3, other arithmetic, orthonormal(): lax.linalg.triangular_solve(factor, left_rows, left_side=False, lower=Tru...  20.5 us
  transfers between devices with their start and end apart: 3, of which 3 were waited for; matrix products, arithmetic and copies ran while one was open for 0% of the time, Pallas kernels for 0%

commit v1 on v0

v1 whole, which is shorter than its diff:
```python
import functools

import jax
import jax.numpy as jnp
from jax import lax
from jax.experimental import pallas as pl
from jax.experimental.pallas import tpu as pltpu
from jax.sharding import PartitionSpec as P

M_ROWS = 8192
N_COLS = 26624
RANK = 256
SCALE = (M_ROWS * N_COLS / RANK) ** 0.5
F32, BF16 = jnp.float32, jnp.bfloat16
PANEL = 64
VMEM = pl.BlockSpec(memory_space=pltpu.VMEM)
ROWS_BY_ROWS = (((0,), (0,)), ((), ()))
COLS_BY_COLS = (((1,), (1,)), ((), ()))


def iota(shape, dim):
    return lax.broadcasted_iota(jnp.int32, shape, dim)


def shape(dims, dtype=F32):
    return jax.ShapeDtypeStruct(dims, dtype)


def call(body, out, name, *args, scratch=(), limit=24 << 20, flops=0):
    many = isinstance(out, (list, tuple))
    outs = out if many else [out]
    size = sum(a.size * a.dtype.itemsize for a in (*args, *outs))
    return pl.pallas_call(
        body,
        out_shape=out,
        in_specs=[VMEM] * len(args),
        out_specs=[VMEM] * len(outs) if many else VMEM,
        scratch_shapes=list(scratch),
        compiler_params=pltpu.CompilerParams(vmem_limit_bytes=limit),
        cost_estimate=pl.CostEstimate(flops=flops, bytes_accessed=size, transcendentals=0),
        name=name,
    )(*args)


def split(value):
    high = value.astype(BF16)
    rest = value - high.astype(F32)
    mid = rest.astype(BF16)
    return high, mid, (rest - mid.astype(F32)).astype(BF16)


def left_terms(value, axis):
    high, mid, low = split(value)
    return jnp.concatenate([high, high, mid, mid, high, low], axis=axis)


def right_terms(value):
    high, mid, low = split(value)
    return jnp.concatenate([high, mid, high, mid, low, high], axis=0)


def blend_body(momentum_ref, gradient_ref, basis_ref, blended_ref, left_ref):
    blended = (momentum_ref[...].astype(F32) + gradient_ref[...].astype(F32)).astype(BF16)
    blended_ref[...] = blended
    left_ref[...] = jnp.dot(blended, basis_ref[...], preferred_element_type=F32).astype(BF16)


def blend(momentum, gradient, basis):
    rows, cols = momentum.shape
    rank = basis.shape[1]
    steps = 4
    block = rows // steps
    tile = pl.BlockSpec((block, cols), lambda i: (i, 0))
    return pl.pallas_call(
        blend_body,
        grid=(steps,),
        in_specs=[tile, tile, pl.BlockSpec((cols, rank), lambda i: (0, 0))],
        out_specs=[tile, pl.BlockSpec((block, rank), lambda i: (i, 0))],
        out_shape=[shape((rows, cols), BF16), shape((rows, rank), BF16)],
        compiler_params=pltpu.CompilerParams(vmem_limit_bytes=58 << 20),
        name="blend",
    )(momentum, gradient, basis)


def left_sum_body(parts_ref, out_ref):
    total = parts_ref[0].astype(F32)
    for i in range(1, parts_ref.shape[0]):
        total = total + parts_ref[i].astype(F32)
    low = total.astype(BF16)
    for i in range(out_ref.shape[0]):
        out_ref[i] = low


def project_body(blended_ref, left_ref, out_ref, work_ref):
    parts = out_ref.shape[0]
    rank = left_ref.shape[1]
    some = rank // parts
    block = blended_ref.shape[1] // parts
    left = left_ref[...]
    gram = split(lax.dot_general(left, left, ROWS_BY_ROWS, preferred_element_type=F32))
    work_ref[...] = lax.dot_general(blended_ref[...], left, ROWS_BY_ROWS, preferred_element_type=F32)
    for f in range(parts):
        for i, term in enumerate(gram):
            out_ref[f, i * some : (i + 1) * some, :] = term[f * some : (f + 1) * some]
        out_ref[f, 3 * some :, :] = work_ref[f * block : (f + 1) * block, :].astype(BF16)


def project_sum_body(parts_ref, gram_ref, proj_ref):
    some = gram_ref.shape[1]
    total = parts_ref[0].astype(F32)
    for i in range(1, parts_ref.shape[0]):
        total = total + parts_ref[i].astype(F32)
    gram = (total[2 * some : 3 * some] + total[some : 2 * some]) + total[:some]
    low = total[3 * some :].astype(BF16)
    for i in range(gram_ref.shape[0]):
        gram_ref[i] = gram
        proj_ref[i] = low


def diag_inverse(block):
    b = block.shape[0]
    n, width = b // 8, 2 * b
    eye = iota((b, b), 0) == iota((b, b), 1)
    aug = jnp.concatenate([block, jnp.where(eye, 1.0, 0.0)], axis=1)
    sub = iota((8, width), 0)
    rows = [aug[8 * i : 8 * i + 8] for i in range(n)]
    for g in range(n):
        cols = [
            [jnp.broadcast_to(rows[v][:, 8 * g + k : 8 * g + k + 1], (8, width)) for v in range(g, n)] for k in range(8)
        ]
        own, pivots, scaled = rows[g], jnp.zeros((8, width), F32), []
        for m in range(8):
            pivot = jnp.broadcast_to(cols[m][0][m : m + 1], (8, width))
            pivots = jnp.where(sub == m, pivot, pivots)
            inverse = 1.0 / pivot
            scaled.append(jnp.broadcast_to(own[m : m + 1], (8, width)) * inverse)
            factor = jnp.where(sub > m, cols[m][0], 0.0)
            own = own - factor * scaled[m]
            for k in range(m + 1, 8):
                ratio = jnp.broadcast_to(cols[k][0][m : m + 1], (8, width)) * inverse
                cols[k][0] = cols[k][0] - factor * ratio
                for v in range(1, n - g):
                    cols[k][v] = cols[k][v] - cols[m][v] * ratio
        rows[g] = own * lax.rsqrt(pivots)
        for v in range(1, n - g):
            row = rows[g + v]
            for m in range(8):
                row = row - cols[m][v] * scaled[m]
            rows[g + v] = row
    return jnp.concatenate(rows, axis=0)[:, b:]


def inverse_factor_body(gram_ref, left_ref, inv_ref, ortho_ref):
    rank = gram_ref.shape[0]
    row, col = iota((rank, rank), 0), iota((rank, rank), 1)
    inv_ref[...] = gram_ref[...] + jnp.where(row == col, 0.001, 0.0)
    lanes = iota((1, rank), 1)
    for p in range(0, rank, PANEL):
        q = p + PANEL
        inverse = diag_inverse(inv_ref[p:q, p:q])
        full = jnp.dot(left_terms(inverse, 1), right_terms(inv_ref[p:q, :]), preferred_element_type=F32)
        pieces = [full[:, :p]] if p else []
        pieces.append(inverse)
        if q < rank:
            pieces.append(full[:, q:])
        panel = jnp.concatenate(pieces, axis=1)
        inv_ref[p:q, :] = panel
        if q < rank:
            change = lax.dot_general(
                left_terms(panel[:, q:], 0), right_terms(panel), ROWS_BY_ROWS, preferred_element_type=F32
            )
            inv_ref[q:, :] = jnp.where((lanes >= p) & (lanes < q), 0.0, inv_ref[q:, :]) - change
    inverse = jnp.where(row >= col, inv_ref[...], 0.0)
    inv_ref[...] = inverse
    ortho_ref[...] = by_inverse(left_ref[...], inverse).astype(BF16)


def by_inverse(low, inverse):
    n = inverse.shape[0]
    parts = lax.dot_general(low, jnp.concatenate(split(inverse), axis=0), COLS_BY_COLS, preferred_element_type=F32)
    return parts[:, :n] + (parts[:, n : 2 * n] + parts[:, 2 * n :])


def right_body(proj_ref, inv_ref, right_ref, low_ref, colsq_ref):
    right = by_inverse(proj_ref[...], inv_ref[...])
    right_ref[...] = right
    low_ref[...] = right.astype(BF16)
    colsq_ref[...] = jnp.broadcast_to(jnp.sum(right * right, axis=0)[None, None, :], colsq_ref.shape)


def feedback_body(blended_ref, ortho_ref, low_ref, momentum_ref):
    feedback = lax.dot_general(ortho_ref[...], low_ref[...], COLS_BY_COLS, preferred_element_type=F32)
    momentum_ref[...] = (blended_ref[...].astype(F32) - 0.1 * feedback).astype(BF16)


def feedback(blended, ortho, low):
    rows, cols = blended.shape
    rank = ortho.shape[1]
    steps = 4
    block = rows // steps
    tile = pl.BlockSpec((block, cols), lambda i: (i, 0))
    return pl.pallas_call(
        feedback_body,
        grid=(steps,),
        in_specs=[tile, pl.BlockSpec((block, rank), lambda i: (i, 0)), pl.BlockSpec((cols, rank), lambda i: (0, 0))],
        out_specs=tile,
        out_shape=shape((rows, cols), BF16),
        compiler_params=pltpu.CompilerParams(vmem_limit_bytes=24 << 20),
        name="feedback",
    )(blended, ortho, low)


def update_body(ortho_ref, right_ref, colsq_ref, update_ref, basis_ref):
    @pl.when(pl.program_id(0) == 0)
    def _():
        colsq = colsq_ref[0, 0:1, :]
        for i in range(1, colsq_ref.shape[0]):
            colsq = colsq + colsq_ref[i, 0:1, :]
        basis_ref[...] = (right_ref[...] * lax.rsqrt(colsq + 1e-06)).astype(BF16)

    product = lax.dot_general(ortho_ref[...], basis_ref[...], COLS_BY_COLS, preferred_element_type=F32)
    update_ref[...] = (SCALE * product).astype(BF16)


def update(ortho, right, colsq):
    rows, rank = ortho.shape
    cols = right.shape[0]
    steps = 4
    block = rows // steps
    return pl.pallas_call(
        update_body,
        grid=(steps,),
        in_specs=[
            pl.BlockSpec((block, rank), lambda i: (i, 0)),
            pl.BlockSpec((cols, rank), lambda i: (0, 0)),
            pl.BlockSpec(colsq.shape, lambda i: (0, 0, 0)),
        ],
        out_specs=[pl.BlockSpec((block, cols), lambda i: (i, 0)), pl.BlockSpec((cols, rank), lambda i: (0, 0))],
        out_shape=[shape((rows, cols), BF16), shape((cols, rank), BF16)],
        compiler_params=pltpu.CompilerParams(vmem_limit_bytes=24 << 20),
        name="update",
    )(ortho, right, colsq)


def on_device(momentum, gradient, basis, n_fsdp, n_tp):
    rank = basis.shape[1]
    rows, cols = momentum.shape
    some, block = rank // n_fsdp, cols // n_fsdp

    def exchange(parts, axis):
        return lax.all_to_all(parts, axis, 0, 0, tiled=True)

    blended, left = blend(momentum, gradient, basis)
    parts = exchange(left.reshape(n_tp, rows // n_tp, rank), "tp")
    spread = call(left_sum_body, shape(parts.shape, BF16), "left_sum", parts)
    left = exchange(spread, "tp").reshape(rows, rank)

    sent = shape((n_fsdp, 3 * some + block, rank), BF16)
    parts = call(project_body, sent, "project", blended, left, scratch=[pltpu.VMEM((cols, rank), F32)])
    gram, proj = call(
        project_sum_body,
        [shape((n_fsdp, some, rank)), shape((n_fsdp, block, rank), BF16)],
        "project_sum",
        exchange(parts, "fsdp"),
    )
    gram, proj = lax.optimization_barrier((exchange(gram, "fsdp"), proj))
    inverse, ortho = call(
        inverse_factor_body,
        [shape((rank, rank)), shape((rows, rank), BF16)],
        "inverse_factor",
        gram.reshape(rank, rank),
        left,
        flops=10**10,
    )
    right, low, colsq = call(
        right_body,
        [shape((cols, rank)), shape((cols, rank), BF16), shape((n_tp, 8, rank))],
        "right",
        exchange(proj, "fsdp").reshape(cols, rank),
        inverse,
    )
    colsq = exchange(colsq, "tp")
    momentum_next = feedback(blended, ortho, low)
    update_next, basis_next = update(ortho, right, colsq)
    return momentum_next, basis_next, update_next


def solution(mesh):
    body = functools.partial(on_device, n_fsdp=mesh.shape["fsdp"], n_tp=mesh.shape["tp"])
    return jax.shard_map(
        body,
        mesh=mesh,
        in_specs=(P("fsdp", "tp"), P("fsdp", "tp"), P("tp", None)),
        out_specs=(P("fsdp", "tp"), P("tp", None), P("fsdp", "tp")),
        check_vma=False,
    )
```

time: 430 us -> 121 us (0.28)
  waiting for transfers between devices: 306 us -> 6.62 us
  other arithmetic: 58.5 us -> 0 us
  blocking collectives: 25.7 us -> 72.3 us
  Pallas kernels: 0 us -> 23.2 us
  matrix products: 15.5 us -> 0 us
  between operations: 15.3 us -> 0.69 us
  starting transfers between devices: 0.12 us -> 10.3 us
    psum x3 -> x0, waiting for transfers between devices: 306 us -> none  [the longest x1 113 us: on_device(): lax.psum(jnp.dot(blended, basis, preferred_element_type=jnp.float32), 'tp')]
    all_to_all x0 -> x4, blocking collectives: none -> 72.3 us  [exchange(): return lax.all_to_all(parts, axis, 0, 0, tiled=True)]
    another operation x9 -> x0, other arithmetic: 54.6 us -> none  [the longest x6 34 us: orthonormal(): factor = jnp.linalg.cholesky(gram)]
    psum x1 -> x0, blocking collectives: 25.7 us -> none  [on_device(): colsq = lax.psum(jnp.sum(right * right, axis=0), 'tp')]
    pallas_call x0 -> x8, Pallas kernels: none -> 23.2 us  [the longest x5 12.8 us: call(): pl.pallas_call(body, out_shape=out, in_specs=[VMEM] * len(args), out_spec...]
    dot_general x5 -> x0, matrix products: 13.6 us -> none  [the longest x1 3.41 us: on_device(): jnp.dot(blended, basis, preferred_element_type=jnp.float32)]
    all_to_all x0 -> x2, starting transfers between devices: none -> 10.3 us  [exchange(): return lax.all_to_all(parts, axis, 0, 0, tiled=True)]
    all_to_all x0 -> x2, waiting for transfers between devices: none -> 6.62 us  [exchange(): return lax.all_to_all(parts, axis, 0, 0, tiled=True)]
  transfers between devices with their start and end apart: 3 -> 2, of which waited for: 3 -> 2; matrix products, arithmetic and copies ran while one was open for 0% -> 0% of each run, Pallas kernels for 0% -> 10%
where the time goes in v1:
time: 121 us; the launch traced here: 120 us
  blocking collectives  72.3 us (60%)
  Pallas kernels  23.2 us (19%)
  starting transfers between devices  10.3 us (9%)
  local copies, waits for them, and re-layouts  7.32 us (6%)
  waiting for transfers between devices  6.62 us (5%)
    all_to_all x4, blocking collectives, exchange(): return lax.all_to_all(parts, axis, 0, 0, tiled=True)  72.3 us
    pallas_call x5, Pallas kernels, call(): pl.pallas_call(body, out_shape=out, in_specs=[VMEM] * len(args), out_spec...  12.8 us
    all_to_all x2, starting transfers between devices, exchange(): return lax.all_to_all(parts, axis, 0, 0, tiled=True)  10.3 us
    unnamed x18, local copies, waits for them, and re-layouts  7.32 us
    all_to_all x2, waiting for transfers between devices, exchange(): return lax.all_to_all(parts, axis, 0, 0, tiled=True)  6.62 us
    pallas_call x1, Pallas kernels, blend(): pl.pallas_call(blend_body, grid=(steps,), in_specs=[tile, tile, pl.BlockS...  4.5 us
    pallas_call x1, Pallas kernels, update(): pl.pallas_call(update_body, grid=(steps,), in_specs=[pl.BlockSpec((block,...  3.03 us
    pallas_call x1, Pallas kernels, feedback(): pl.pallas_call(feedback_body, grid=(steps,), in_specs=[tile, pl.BlockSpec...  2.78 us
  transfers between devices with their start and end apart: 2, of which 2 were waited for; matrix products, arithmetic and copies ran while one was open for 0% of the time, Pallas kernels for 10%

profile of v1, /device:TPU:1, one launch (start us, length us, event | category | flops | bytes accessed | tf_op | source)
XLA Modules:
  0.0 120.4 jit_solution(5528793815554276508)
XLA Ops:
  0.6 4.5 %blend.1 = (bf16[512,1664]{1,0:T(8,128)(2,1)}, bf16[512,256]{1,0:T(8,128)(2,1)}) custom-call(bf16[512,1664]{1,0:T(8,128)(2,1)} %momentum_ref.1, bf16[512,1664]{1,0:T(8,128)(2,1)} %gradient_ref.1, bf16[1664,256]{1,0:T(8,128)(2,1)} %basis_ref.1), custom_call_target="tpu_custom_call" | custom-call | tf_op jit(solution)/shard_map/blend/pallas_call | solution.py:74
  5.1 21.7 %all_to_all.30.parts_ref = bf16[16,32,256]{2,1,0:T(8,128)(2,1)S(1)} all-to-all(bf16[16,32,256]{2,1,0:T(8,128)(2,1)} %bitcast.8), channel_id=1, replica_groups=mesh['fsdp'=16,'tp'=16] {'tp'}, dimensions={0} | all-to-all | bytes 524288 | tf_op jit(solution)/shard_map/all_to_all | solution.py:251
  26.9 14.4 %all_to_all.31 = bf16[16,32,256]{2,1,0:T(8,128)(2,1)S(1)} all-to-all(bf16[16,32,256]{2,1,0:T(8,128)(2,1)S(1)} %left_sum.1), channel_id=1, replica_groups=mesh['fsdp'=16,'tp'=16] {'tp'}, dimensions={0} | all-to-all | bytes 524288 | tf_op jit(solution)/shard_map/all_to_all | solution.py:251
  41.3 0.0 copy-start
  41.3 1.5 %copy-done = bf16[512,1664]{1,0:T(8,128)(2,1)S(1)} copy-done((bf16[512,1664]{1,0:T(8,128)(2,1)S(1)}, bf16[512,1664]{1,0:T(8,128)(2,1)}, u32[]{:S(2)}) %copy-start) | copy-done | bytes 1703960
  42.7 0.7 project.1
  43.4 25.3 %all_to_all.32.parts_ref = bf16[16,152,256]{2,1,0:T(8,128)(2,1)S(1)} all-to-all(bf16[16,152,256]{2,1,0:T(8,128)(2,1)S(1)} %project.1), channel_id=1, replica_groups=mesh['fsdp'=16,'tp'=16] {'fsdp'}, dimensions={0} | all-to-all | bytes 2490368 | tf_op jit(solution)/shard_map/all_to_all | solution.py:251
  68.8 1.0 project_sum.1
  69.8 10.9 %all_to_all.33 = f32[16,16,256]{2,1,0:T(8,128)S(1)} all-to-all(f32[16,16,256]{2,1,0:T(8,128)S(1)} %get-tuple-element.18), channel_id=1, replica_groups=mesh['fsdp'=16,'tp'=16] {'fsdp'}, dimensions={0} | all-to-all | bytes 524288 | tf_op jit(solution)/shard_map/all_to_all | solution.py:251
  80.7 3.6 %all-to-all-start.4 = ((bf16[16,104,256]{2,1,0:T(8,128)(2,1)}), bf16[16,104,256]{2,1,0:T(8,128)(2,1)S(1)}, u32[]{:S(2)}, u32[]{:S(2)}) async-start(bf16[16,104,256]{2,1,0:T(8,128)(2,1)} %get-tuple-element.22), calls=%async_computation.4 | async-start | bytes 1703936 | tf_op jit(solution)/shard_map/all_to_all | solution.py:251
  84.3 0.0 copy-start.1
  84.3 9.5 %inverse_factor.1 = (f32[256,256]{1,0:T(8,128)S(1)}, bf16[512,256]{1,0:T(8,128)(2,1)S(1)}) custom-call(f32[256,256]{1,0:T(8,128)S(1)} %bitcast.7, bf16[512,256]{1,0:T(8,128)(2,1)S(1)} %bitcast.6), custom_call_target="tpu_custom_call" | custom-call | flops 10000000000 | bytes 1048576 | tf_op jit(solution)/shard_map/inverse_factor/pallas_call | solution.py:33
  93.9 0.0 copy-start.4
  93.9 0.7 copy-done.4
  94.6 2.3 %all-to-all-done.4 = bf16[16,104,256]{2,1,0:T(8,128)(2,1)S(1)} async-done(((bf16[16,104,256]{2,1,0:T(8,128)(2,1)}), bf16[16,104,256]{2,1,0:T(8,128)(2,1)S(1)}, u32[]{:S(2)}, u32[]{:S(2)}) %all-to-all-start.4) | async-done | bytes 852000 | tf_op jit(solution)/shard_map/all_to_all | solution.py:251
  96.9 1.5 %right.1 = (f32[1664,256]{1,0:T(8,128)S(1)}, bf16[1664,256]{1,0:T(8,128)(2,1)S(1)}, f32[16,8,256]{2,1,0:T(8,128)}) custom-call(bf16[1664,256]{1,0:T(8,128)(2,1)S(1)} %bitcast.4, f32[256,256]{1,0:T(8,128)S(1)} %get-tuple-element.23.inv_ref), custom_call_target="tpu_custom_call" | custom-call | bytes 3801088 | tf_op jit(solution)/shard_map/right/pallas_call | solution.py:33
  98.4 0.0 copy-start.2
  98.4 1.2 %copy-done.2 = f32[1664,256]{1,0:T(8,128)} copy-done((f32[1664,256]{1,0:T(8,128)}, f32[1664,256]{1,0:T(8,128)S(1)}, u32[]{:S(2)}) %copy-start.2) | copy-done | bytes 1703960
  99.6 0.0 copy-start.7
  99.6 0.9 copy-done.7
  100.5 6.7 %all-to-all-start.5 = ((f32[16,8,256]{2,1,0:T(8,128)}), f32[16,8,256]{2,1,0:T(8,128)S(1)}, u32[]{:S(2)}, u32[]{:S(2)}) async-start(f32[16,8,256]{2,1,0:T(8,128)} %get-tuple-element.26), calls=%async_computation.5 | async-start | bytes 262144 | tf_op jit(solution)/shard_map/all_to_all | solution.py:251
  107.2 0.0 copy-done.1
  107.2 0.0 copy-start.5
  107.2 0.9 copy-done.5
  108.1 0.0 copy-start.8
  108.1 1.2 copy-done.8
  109.3 0.0 copy-start.3
  109.3 2.8 %feedback.1 = bf16[512,1664]{1,0:T(8,128)(2,1)} custom-call(bf16[512,1664]{1,0:T(8,128)(2,1)S(1)} %copy-done.1, bf16[512,256]{1,0:T(8,128)(2,1)S(1)} %copy-done.5, bf16[1664,256]{1,0:T(8,128)(2,1)S(1)} %copy-done.8), custom_call_target="tpu_custom_call" | custom-call | tf_op jit(solution)/shard_map/feedback/pallas_call | solution.py:202
  112.1 4.3 %all-to-all-done.5.colsq_ref = f32[16,8,256]{2,1,0:T(8,128)S(1)} async-done(((f32[16,8,256]{2,1,0:T(8,128)}), f32[16,8,256]{2,1,0:T(8,128)S(1)}, u32[]{:S(2)}, u32[]{:S(2)}) %all-to-all-start.5) | async-done | bytes 131104 | tf_op jit(solution)/shard_map/all_to_all | solution.py:251
  116.4 0.0 copy-done.3
  116.4 0.0 copy-start.6
  116.4 0.9 copy-done.6
  117.4 3.0 %update.1 = (bf16[512,1664]{1,0:T(8,128)(2,1)}, bf16[1664,256]{1,0:T(8,128)(2,1)}) custom-call(bf16[512,256]{1,0:T(8,128)(2,1)S(1)} %copy-done.6, f32[1664,256]{1,0:T(8,128)S(1)} %copy-done.3, f32[16,8,256]{2,1,0:T(8,128)S(1)} %all-to-all-done.5.colsq_ref), custom_call_target="tpu_custom_call" | custom-call | tf_op jit(solution)/shard_map/update/pallas_call | solution.py:230
  (1 shorter events, 0.0 us)
Async XLA Ops:
  41.3 1.5 %copy-start = (bf16[512,1664]{1,0:T(8,128)(2,1)S(1)}, bf16[512,1664]{1,0:T(8,128)(2,1)}, u32[]{:S(2)}) copy-start(bf16[512,1664]{1,0:T(8,128)(2,1)} %get-tuple-element.16.blended_ref) | copy-start | bytes 5111812
  80.7 16.2 %all-to-all-start.4 = ((bf16[16,104,256]{2,1,0:T(8,128)(2,1)}), bf16[16,104,256]{2,1,0:T(8,128)(2,1)S(1)}, u32[]{:S(2)}, u32[]{:S(2)}) async-start(bf16[16,104,256]{2,1,0:T(8,128)(2,1)} %get-tuple-element.22), calls=%async_computation.4 | async-start | bytes 1703936 | tf_op jit(solution)/shard_map/all_to_all | solution.py:251
  84.3 22.9 %copy-start.1 = (bf16[512,1664]{1,0:T(8,128)(2,1)S(1)}, bf16[512,1664]{1,0:T(8,128)(2,1)}, u32[]{:S(2)}) copy-start(bf16[512,1664]{1,0:T(8,128)(2,1)} %get-tuple-element.16.blended_ref) | copy-start | bytes 5111812
  93.9 0.7 copy-start.4
  98.4 1.2 %copy-start.2 = (f32[1664,256]{1,0:T(8,128)}, f32[1664,256]{1,0:T(8,128)S(1)}, u32[]{:S(2)}) copy-start(f32[1664,256]{1,0:T(8,128)S(1)} %get-tuple-element.25.right_ref) | copy-start | bytes 5111812
  99.6 0.9 copy-start.7
  100.5 15.9 %all-to-all-start.5 = ((f32[16,8,256]{2,1,0:T(8,128)}), f32[16,8,256]{2,1,0:T(8,128)S(1)}, u32[]{:S(2)}, u32[]{:S(2)}) async-start(f32[16,8,256]{2,1,0:T(8,128)} %get-tuple-element.26), calls=%async_computation.5 | async-start | bytes 262144 | tf_op jit(solution)/shard_map/all_to_all | solution.py:251
  107.2 1.0 copy-start.5
  108.1 1.2 copy-start.8
  109.3 7.1 %copy-start.3 = (f32[1664,256]{1,0:T(8,128)S(1)}, f32[1664,256]{1,0:T(8,128)}, u32[]{:S(2)}) copy-start(f32[1664,256]{1,0:T(8,128)} %copy-done.2) | copy-start | bytes 5111812
  116.4 1.0 copy-start.6
